TPU v7x, 512 devices: a whole 4x8x8 slice. The times are simulated.
512 devices in a mesh: box: 128 (over z, y, x_hi), seg: 4 (over x_lo, core).
Axes of the slice: x: 4 (x_hi: 2, x_lo: 2; x = x_hi * 2 + x_lo), y: 8, z: 8, core: 2. Of those that a mesh axis runs over, the one named last changes fastest.
Arguments:
- density_zero: bfloat16 [65536, 64], P('box'), may hold values from 0.25 to 4
- offsets: int32 [256, 4], P('box'), may hold values from -4 to 4, as said below
- start_one: int32 [128, 4, 1024], P('box', 'seg'), may hold values from 0 to 511, as said below
- slot_one: int32 [128, 4, 1024], P('box', 'seg'), may hold values from 0 to 3
- end_one: int32 [128, 4, 1024], P('box', 'seg'), may hold values from 0 to 255
- weight_one: float32 [128, 4, 1024], P('box', 'seg'), may hold values from 0.25 to 4
- start_two: int32 [128, 4, 1024], P('box', 'seg'), may hold values from 0 to 511, as said below
- slot_two: int32 [128, 4, 1024], P('box', 'seg'), may hold values from 0 to 3
- end_two: int32 [128, 4, 1024], P('box', 'seg'), may hold values from 0 to 255
- weight_two: float32 [128, 4, 1024], P('box', 'seg'), may hold values from 0.25 to 4
Outputs:
- density_one: bfloat16 [65536, 64], P('box')
- density_two: bfloat16 [65536, 64], P('box')
Inputs may be any that keep to these rules, and one draw needn't show every extreme that they name: `offsets`: in each row, the 4 entries are distinct. `start_one`: for every [g, l], each of the 512 rows appears exactly 1024 // 512 times. `start_two`: for every [g, l], each of the 512 rows appears exactly 1024 // 512 times.
All inputs are finite; a program needn't handle non-finite values.
Results may differ from a plain program's by a relative error of at most 0.009.
Values may be sent and summed in bfloat16 or wider, within the bound.
No kernel may reach another device: no remote copies, remote signals or barrier semaphores. Data moves between devices by JAX's collectives and lax.ppermute only.
A program may use at most 64 MiB of HBM per device.

v0:
```python
import jax
import jax.numpy as jnp
from jax import lax
from jax.sharding import PartitionSpec as P

REACH = 2


def from_behind(block, axis, distance):
    devices = range(lax.axis_size(axis))
    route = [((i - distance) % len(devices), i) for i in devices]
    return lax.ppermute(block, axis, route)


def three_parts(values):
    high = values.astype(jnp.bfloat16)
    rest = values - high.astype(jnp.float32)
    middle = rest.astype(jnp.bfloat16)
    low = (rest - middle.astype(jnp.float32)).astype(jnp.bfloat16)
    return (high, middle, low)


def onehot_left(table, values):
    total = None
    for member in three_parts(values):
        term = lax.dot_general(
            table, member, (((0,), (0,)), ((), ())), preferred_element_type=jnp.float32
        )
        total = term if total is None else total + term
    return total


def segment_pushes(start, slot, end, weight, scaled, width_k, block):
    rows, cols = scaled.shape
    blocks_dev = rows // block
    count = start.shape[0]
    step = min(2048, count)
    turns = count // step
    columns = blocks_dev * width_k * block

    def one_piece(acc, index):
        pick = (start[:, None] == jnp.arange(rows, dtype=jnp.int32)[None, :]).astype(jnp.bfloat16)
        fetched = jnp.dot(pick, scaled, preferred_element_type=jnp.float32)
        carried = fetched * weight[:, None]
        target = start // block * (width_k * block) + slot * block + end
        place = (target[:, None] == jnp.arange(columns, dtype=jnp.int32)[None, :]).astype(
            jnp.bfloat16
        )
        return (acc + onehot_left(place, carried), None)

    total, unused = lax.scan(one_piece, jnp.zeros((columns, cols), jnp.float32), jnp.arange(turns))
    return total.reshape(blocks_dev, width_k, block, cols)


def place_blocks(pushes, offsets):
    blocks_dev, width_k = offsets.shape
    span = 2 * REACH + 1
    target = jnp.arange(blocks_dev, dtype=jnp.int32)[:, None] + offsets + REACH * blocks_dev
    placing = (
        target[:, :, None] == jnp.arange(span * blocks_dev, dtype=jnp.int32)[None, None, :]
    ).astype(jnp.float32)
    return (placing, jnp.einsum("jku,jkec->uec", placing, pushes, precision=lax.Precision.HIGHEST))


def push_lanes(density, totals, start, slot, end, weight, offsets):
    rows, cols = density.shape
    blocks_dev, width_k = offsets.shape
    block = rows // blocks_dev
    span = 2 * REACH + 1
    scaled = (density.astype(jnp.float32) / totals[:, None]).astype(jnp.bfloat16)
    pushes = segment_pushes(start, slot, end, weight, scaled, width_k, block)
    placing, stacked = place_blocks(pushes, offsets)
    stacked = stacked.reshape(span, -1, 128)
    summed = lax.psum(stacked, "seg")
    combined = summed[REACH]
    for delta in range(-REACH, REACH + 1):
        if delta != 0:
            combined = combined + from_behind(summed[delta + REACH], "box", delta)
    return combined.reshape(rows, cols).astype(jnp.bfloat16)


def body(
    density_zero,
    offsets,
    start_one,
    slot_one,
    end_one,
    weight_one,
    start_two,
    slot_two,
    end_two,
    weight_two,
):
    rows = density_zero.shape[0]
    days = ((start_one, slot_one, end_one, weight_one), (start_two, slot_two, end_two, weight_two))
    flat = [tuple((member.reshape(-1) for member in day)) for day in days]
    density = density_zero
    results = []
    partial_totals = jnp.stack(
        [jax.ops.segment_sum(day[3], day[0], num_segments=rows) for day in flat]
    )
    totals = lax.psum(partial_totals, "seg")
    for number in range(2):
        starts, slots, ends, weights = flat[number]
        density = push_lanes(density, totals[number], starts, slots, ends, weights, offsets)
        results.append(density)
    return (results[0], results[1])


def solution(mesh):
    placed = (
        P("box", None),
        P("box", None),
        P("box", "seg", None),
        P("box", "seg", None),
        P("box", "seg", None),
        P("box", "seg", None),
        P("box", "seg", None),
        P("box", "seg", None),
        P("box", "seg", None),
        P("box", "seg", None),
    )
    return jax.shard_map(
        body,
        mesh=mesh,
        in_specs=placed,
        out_specs=(P("box", None), P("box", None)),
        check_vma=False,
    )
```

profile of v0, /device:TPU:1, one launch (start us, length us, event | category | flops | bytes accessed | tf_op | source)
XLA Modules:
  0.0 211.3 jit_solution(17053488340971013685)
XLA Ops:
  7.2 0.0 all-reduce.3.cloned.1.call-start
  7.2 0.7 add_add_fusion
  7.9 7.8 %scatter_custom_fusion = f32[512]{0:T(512)S(1)} fusion(s32[1024]{0:T(1024)} %bitcast.73, f32[1024]{0:T(1024)} %bitcast.82, f32[]{:T(128)} %constant.47.clone.1), kind=kCustom, calls=%fused_computation.91 | custom fusion | flops 1024 | bytes 2560 | tf_op jit(solution)/shard_map/scatter-add | solution.py:100
  15.7 7.8 %scatter_custom_fusion.1 = f32[512]{0:T(512)S(1)} fusion(s32[1024]{0:T(1024)} %bitcast.77, f32[1024]{0:T(1024)} %bitcast.84, f32[]{:T(128)} %constant.47.clone.1), kind=kCustom, calls=%fused_computation.89 | custom fusion | flops 1024 | bytes 2560 | tf_op jit(solution)/shard_map/scatter-add | solution.py:100
  23.4 11.9 %psum.21 = f32[2,512]{1,0:T(2,128)S(1)} all-reduce(f32[2,512]{1,0:T(2,128)S(1)} %pad_maximum_fusion), channel_id=1, replica_groups=mesh['box'=128,'seg'=4] {'seg'}, use_global_device_ids=true, to_apply=%region_2.0 | all-reduce | flops 1024 | bytes 8192 | tf_op jit(solution)/shard_map/psum | solution.py:102
  35.3 0.7 broadcast_multiply_fusion.1
  36.0 0.7 fusion.43
  36.7 1.5 fusion.19
  38.2 1.8 fusion.4
  40.0 1.6 fusion.12
  41.6 1.8 fusion.13
  43.4 0.4 reshape.136
  43.7 0.7 convolution_bitcast_fusion.1
  44.5 0.5 copy.12
  45.0 1.1 reshape.137
  46.1 0.0 all-reduce.3.cloned.1.call-update
  46.1 0.0 all-reduce.5.cloned.1.call-start
  46.2 50.1 %all-reduce.3.cloned.1.call-done = f32[5,256,128]{2,1,0:T(8,128)} async-done(((f32[5,256,128]{2,1,0:T(8,128)}), f32[5,256,128]{2,1,0:T(8,128)}) %all-reduce.3.cloned.1.call-update) | async-done | bytes 655376 | tf_op jit(solution)/shard_map/psum | solution.py:74
  96.3 1.1 slice_bitcast_fusion.8
  97.4 7.5 %collective-permute-start = (f32[256,128]{1,0:T(8,128)S(1)}, f32[256,128]{1,0:T(8,128)S(1)}, u32[]{:S(2)}, u32[]{:S(2)}) collective-permute-start(f32[256,128]{1,0:T(8,128)S(1)} %get-tuple-element.48), channel_id=1, source_target_pairs={{8,0},{12,4},{16,8},{20,12},{24,16},{28,20},{32,24},{36,28},{40,32... | collective-permute-start | bytes 393224 | tf_op jit(solution)/shard_map/ppermute | solution.py:12
  105.0 1.9 collective-permute-start.3
  106.9 4.3 %collective-permute-start.2 = (f32[256,128]{1,0:T(8,128)S(1)}, f32[256,128]{1,0:T(8,128)S(1)}, u32[]{:S(2)}, u32[]{:S(2)}) collective-permute-start(f32[256,128]{1,0:T(8,128)S(1)} %get-tuple-element.50), channel_id=1, source_target_pairs={{508,0},{0,4},{4,8},{8,12},{12,16},{16,20},{20,24},{24,28},{28,32}... | collective-permute-start | bytes 393224 | tf_op jit(solution)/shard_map/ppermute | solution.py:12
  111.2 6.9 %collective-permute-start.1 = (f32[256,128]{1,0:T(8,128)S(1)}, f32[256,128]{1,0:T(8,128)S(1)}, u32[]{:S(2)}, u32[]{:S(2)}) collective-permute-start(f32[256,128]{1,0:T(8,128)S(1)} %get-tuple-element.51), channel_id=1, source_target_pairs={{4,0},{8,4},{12,8},{16,12},{20,16},{24,20},{28,24},{32,28},{36,32}... | collective-permute-start | bytes 393224 | tf_op jit(solution)/shard_map/ppermute | solution.py:12
  118.2 1.9 collective-permute-done.2
  120.1 2.2 %collective-permute-done.1 = f32[256,128]{1,0:T(8,128)S(1)} collective-permute-done((f32[256,128]{1,0:T(8,128)S(1)}, f32[256,128]{1,0:T(8,128)S(1)}, u32[]{:S(2)}, u32[]{:S(2)}) %collective-permute-start.1) | collective-permute-done | bytes 131104 | tf_op jit(solution)/shard_map/ppermute | solution.py:12
  122.3 1.0 fusion.37
  123.2 0.1 convert_element_type.82
  123.3 0.7 fusion.18
  124.0 1.8 fusion.1
  125.8 1.6 fusion.14
  127.4 1.8 fusion.15
  129.2 0.4 reshape.139
  129.5 0.7 convolution_bitcast_fusion
  130.3 0.5 copy.13
  130.8 1.1 reshape.140
  131.9 0.0 all-reduce.5.cloned.1.call-update
  131.9 44.8 %all-reduce.5.cloned.1.call-done = f32[5,256,128]{2,1,0:T(8,128)} async-done(((f32[5,256,128]{2,1,0:T(8,128)}), f32[5,256,128]{2,1,0:T(8,128)}) %all-reduce.5.cloned.1.call-update) | async-done | bytes 655376 | tf_op jit(solution)/shard_map/psum | solution.py:74
  176.7 1.1 slice_bitcast_fusion.3
  177.9 7.5 %collective-permute-start.4 = (f32[256,128]{1,0:T(8,128)S(1)}, f32[256,128]{1,0:T(8,128)S(1)}, u32[]{:S(2)}, u32[]{:S(2)}) collective-permute-start(f32[256,128]{1,0:T(8,128)S(1)} %get-tuple-element.36), channel_id=1, source_target_pairs={{8,0},{12,4},{16,8},{20,12},{24,16},{28,20},{32,24},{36,28},{40,32... | collective-permute-start | bytes 393224 | tf_op jit(solution)/shard_map/ppermute | solution.py:12
  185.4 1.9 collective-permute-start.7
  187.3 4.3 %collective-permute-start.6 = (f32[256,128]{1,0:T(8,128)S(1)}, f32[256,128]{1,0:T(8,128)S(1)}, u32[]{:S(2)}, u32[]{:S(2)}) collective-permute-start(f32[256,128]{1,0:T(8,128)S(1)} %get-tuple-element.38), channel_id=1, source_target_pairs={{508,0},{0,4},{4,8},{8,12},{12,16},{16,20},{20,24},{24,28},{28,32}... | collective-permute-start | bytes 393224 | tf_op jit(solution)/shard_map/ppermute | solution.py:12
  191.7 6.7 %collective-permute-start.5 = (f32[256,128]{1,0:T(8,128)S(1)}, f32[256,128]{1,0:T(8,128)S(1)}, u32[]{:S(2)}, u32[]{:S(2)}) collective-permute-start(f32[256,128]{1,0:T(8,128)S(1)} %get-tuple-element.39), channel_id=1, source_target_pairs={{4,0},{8,4},{12,8},{16,12},{20,16},{24,20},{28,24},{32,28},{36,32}... | collective-permute-start | bytes 393224 | tf_op jit(solution)/shard_map/ppermute | solution.py:12
  198.4 0.7 copy.14
  199.1 1.4 collective-permute-done.6
  200.5 2.2 %collective-permute-done.5 = f32[256,128]{1,0:T(8,128)S(1)} collective-permute-done((f32[256,128]{1,0:T(8,128)S(1)}, f32[256,128]{1,0:T(8,128)S(1)}, u32[]{:S(2)}, u32[]{:S(2)}) %collective-permute-start.5) | collective-permute-done | bytes 131104 | tf_op jit(solution)/shard_map/ppermute | solution.py:12
  202.7 0.9 fusion.32
  203.6 0.1 convert_element_type.91
  203.7 0.7 copy.15
  (16 shorter events, 0.1 us)
Async XLA Ops:
  7.2 89.1 %all-reduce.3.cloned.1.call-start = ((), (), s32[]{:S(2)}) async-start(), calls=%async_computation | async-start | bytes 1310720 | tf_op jit(solution)/shard_map/psum | solution.py:74
  45.0 1.2 copy-start
  46.1 72.0 %copy-start.1 = (s32[1,1,1024]{2,1,0:T(1,128)S(1)}, s32[1,1,1024]{2,1,0:T(1,128)}, u32[]{:S(2)}) copy-start(s32[1,1,1024]{2,1,0:T(1,128)} %param.18) | copy-start | bytes 12292
  46.1 72.0 %copy-start.2 = (s32[1,1,1024]{2,1,0:T(1,128)S(1)}, s32[1,1,1024]{2,1,0:T(1,128)}, u32[]{:S(2)}) copy-start(s32[1,1,1024]{2,1,0:T(1,128)} %param.16) | copy-start | bytes 12292
  46.1 77.2 %copy-start.3 = (f32[1,1,1024]{2,1,0:T(1,128)S(1)}, f32[1,1,1024]{2,1,0:T(1,128)}, u32[]{:S(2)}) copy-start(f32[1,1,1024]{2,1,0:T(1,128)} %param.19) | copy-start | bytes 12292
  46.1 130.6 %all-reduce.5.cloned.1.call-start = ((), (), s32[]{:S(2)}) async-start(), calls=%async_computation.1 | async-start | bytes 1310720 | tf_op jit(solution)/shard_map/psum | solution.py:74
  97.4 20.7 %collective-permute-start = (f32[256,128]{1,0:T(8,128)S(1)}, f32[256,128]{1,0:T(8,128)S(1)}, u32[]{:S(2)}, u32[]{:S(2)}) collective-permute-start(f32[256,128]{1,0:T(8,128)S(1)} %get-tuple-element.48), channel_id=1, source_target_pairs={{8,0},{12,4},{16,8},{20,12},{24,16},{28,20},{32,24},{36,28},{40,32... | collective-permute-start | bytes 393224 | tf_op jit(solution)/shard_map/ppermute | solution.py:12
  105.0 13.2 %collective-permute-start.3 = (f32[256,128]{1,0:T(8,128)S(1)}, f32[256,128]{1,0:T(8,128)S(1)}, u32[]{:S(2)}, u32[]{:S(2)}) collective-permute-start(f32[256,128]{1,0:T(8,128)S(1)} %get-tuple-element.49), channel_id=1, source_target_pairs={{504,0},{508,4},{0,8},{4,12},{8,16},{12,20},{16,24},{20,28},{24,32... | collective-permute-start | bytes 393224 | tf_op jit(solution)/shard_map/ppermute | solution.py:12
  106.9 13.2 %collective-permute-start.2 = (f32[256,128]{1,0:T(8,128)S(1)}, f32[256,128]{1,0:T(8,128)S(1)}, u32[]{:S(2)}, u32[]{:S(2)}) collective-permute-start(f32[256,128]{1,0:T(8,128)S(1)} %get-tuple-element.50), channel_id=1, source_target_pairs={{508,0},{0,4},{4,8},{8,12},{12,16},{16,20},{20,24},{24,28},{28,32}... | collective-permute-start | bytes 393224 | tf_op jit(solution)/shard_map/ppermute | solution.py:12
  111.2 11.0 %collective-permute-start.1 = (f32[256,128]{1,0:T(8,128)S(1)}, f32[256,128]{1,0:T(8,128)S(1)}, u32[]{:S(2)}, u32[]{:S(2)}) collective-permute-start(f32[256,128]{1,0:T(8,128)S(1)} %get-tuple-element.51), channel_id=1, source_target_pairs={{4,0},{8,4},{12,8},{16,12},{20,16},{24,20},{28,24},{32,28},{36,32}... | collective-permute-start | bytes 393224 | tf_op jit(solution)/shard_map/ppermute | solution.py:12
  177.9 21.2 %collective-permute-start.4 = (f32[256,128]{1,0:T(8,128)S(1)}, f32[256,128]{1,0:T(8,128)S(1)}, u32[]{:S(2)}, u32[]{:S(2)}) collective-permute-start(f32[256,128]{1,0:T(8,128)S(1)} %get-tuple-element.36), channel_id=1, source_target_pairs={{8,0},{12,4},{16,8},{20,12},{24,16},{28,20},{32,24},{36,28},{40,32... | collective-permute-start | bytes 393224 | tf_op jit(solution)/shard_map/ppermute | solution.py:12
  185.4 13.7 %collective-permute-start.7 = (f32[256,128]{1,0:T(8,128)S(1)}, f32[256,128]{1,0:T(8,128)S(1)}, u32[]{:S(2)}, u32[]{:S(2)}) collective-permute-start(f32[256,128]{1,0:T(8,128)S(1)} %get-tuple-element.37), channel_id=1, source_target_pairs={{504,0},{508,4},{0,8},{4,12},{8,16},{12,20},{16,24},{20,28},{24,32... | collective-permute-start | bytes 393224 | tf_op jit(solution)/shard_map/ppermute | solution.py:12
  187.3 13.2 %collective-permute-start.6 = (f32[256,128]{1,0:T(8,128)S(1)}, f32[256,128]{1,0:T(8,128)S(1)}, u32[]{:S(2)}, u32[]{:S(2)}) collective-permute-start(f32[256,128]{1,0:T(8,128)S(1)} %get-tuple-element.38), channel_id=1, source_target_pairs={{508,0},{0,4},{4,8},{8,12},{12,16},{16,20},{20,24},{24,28},{28,32}... | collective-permute-start | bytes 393224 | tf_op jit(solution)/shard_map/ppermute | solution.py:12
  191.7 11.0 %collective-permute-start.5 = (f32[256,128]{1,0:T(8,128)S(1)}, f32[256,128]{1,0:T(8,128)S(1)}, u32[]{:S(2)}, u32[]{:S(2)}) collective-permute-start(f32[256,128]{1,0:T(8,128)S(1)} %get-tuple-element.39), channel_id=1, source_target_pairs={{4,0},{8,4},{12,8},{16,12},{20,16},{24,20},{28,24},{32,28},{36,32}... | collective-permute-start | bytes 393224 | tf_op jit(solution)/shard_map/ppermute | solution.py:12
Sparse Core Ops, SparseCore 0:
  46.2 50.0 all-reduce.2
  132.0 44.6 all-reduce.4
where the time goes:
time: 212 us; the launch traced here: 211 us
  waiting for transfers between devices  103 us (49%)
  starting transfers between devices  41.2 us (19%)
  other arithmetic  19.5 us (9%)
  between operations  14.3 us (7%)
  matrix products  13.9 us (7%)
  blocking collectives  11.9 us (6%)
  local copies, waits for them, and re-layouts  7.8 us (4%)
    psum x2, waiting for transfers between devices, push_lanes(): summed = lax.psum(stacked, 'seg')  95 us
    ppermute x8, starting transfers between devices, from_behind(): return lax.ppermute(block, axis, route)  41.1 us
    scatter-add x2, other arithmetic, body(): jax.ops.segment_sum(day[3], day[0], num_segments=rows)  15.5 us
    psum x1, blocking collectives, body(): totals = lax.psum(partial_totals, 'seg')  11.9 us
    dot_general x6, matrix products, onehot_left(): lax.dot_general(table, member, (((0,), (0,)), ((), ())), preferred_elemen...  10.3 us
    ppermute x8, waiting for transfers between devices, from_behind(): return lax.ppermute(block, axis, route)  7.71 us
  transfers between devices with their start and end apart: 10, of which 6 were waited for; matrix products, arithmetic and copies ran while one was open for 0% of the time, Pallas kernels for 0%

commit v1 on v0

--- a/solution.py
+++ b/solution.py
@@ -71,7 +71,7 @@
     pushes = segment_pushes(start, slot, end, weight, scaled, width_k, block)
     placing, stacked = place_blocks(pushes, offsets)
     stacked = stacked.reshape(span, -1, 128)
-    summed = lax.psum(stacked, "seg")
+    summed = jnp.sum(lax.all_gather(stacked, "seg"), axis=0)
     combined = summed[REACH]
     for delta in range(-REACH, REACH + 1):
         if delta != 0:

time: 212 us -> 191 us (0.901)
  waiting for transfers between devices: 103 us -> 81.5 us
  local copies, waits for them, and re-layouts: 7.8 us -> 5.62 us
    psum x2 -> x0, waiting for transfers between devices: 95 us -> none  [push_lanes(): summed = lax.psum(stacked, 'seg')]
    all_gather x0 -> x2, waiting for transfers between devices: none -> 73.4 us  [push_lanes(): summed = jnp.sum(lax.all_gather(stacked, 'seg'), axis=0)]
    reduce_sum x0 -> x2, other arithmetic: none -> 3.91 us  [push_lanes(): summed = jnp.sum(lax.all_gather(stacked, 'seg'), axis=0)]
    squeeze x2, local copies, waits for them, and re-layouts: 2.26 us -> 0.07 us  [push_lanes(): combined = combined + from_behind(summed[delta + REACH], 'box', delta)]
    reshape x2 -> x0, local copies, waits for them, and re-layouts: 2.18 us -> none  [push_lanes(): stacked = stacked.reshape(span, -1, 128)]
    another operation x0 -> x2, local copies, waits for them, and re-layouts: none -> 2.17 us  [push_lanes(): summed = jnp.sum(lax.all_gather(stacked, 'seg'), axis=0)]
where the time goes in v1:
time: 191 us
  waiting for transfers between devices  81.5 us (43%)
  starting transfers between devices  41.8 us (22%)
  other arithmetic  21.6 us (11%)
  between operations  14.3 us (7%)
  matrix products  13.9 us (7%)
  blocking collectives  11.9 us (6%)
  local copies, waits for them, and re-layouts  5.62 us (3%)
    all_gather x2, waiting for transfers between devices, push_lanes(): summed = jnp.sum(lax.all_gather(stacked, 'seg'), axis=0)  73.4 us
    ppermute x8, starting transfers between devices, from_behind(): return lax.ppermute(block, axis, route)  41.7 us
    scatter-add x2, other arithmetic, body(): jax.ops.segment_sum(day[3], day[0], num_segments=rows)  15.5 us
    psum x1, blocking collectives, body(): totals = lax.psum(partial_totals, 'seg')  11.9 us
    dot_general x6, matrix products, onehot_left(): lax.dot_general(table, member, (((0,), (0,)), ((), ())), preferred_elemen...  10.3 us
    ppermute x8, waiting for transfers between devices, from_behind(): return lax.ppermute(block, axis, route)  8.03 us
    reduce_sum x2, other arithmetic, push_lanes(): summed = jnp.sum(lax.all_gather(stacked, 'seg'), axis=0)  3.91 us
  transfers between devices with their start and end apart: 10, of which 6 were waited for; matrix products, arithmetic and copies ran while one was open for 0% of the time, Pallas kernels for 0%

profile of v1, /device:TPU:1, one launch (start us, length us, event | category | flops | bytes accessed | tf_op | source)
XLA Modules:
  0.0 190.7 jit_solution(5222708920339940392)
XLA Ops:
  7.2 0.0 all-gather.3.cloned.1.call-start
  7.2 0.7 add_add_fusion
  7.9 7.8 %scatter_custom_fusion = f32[512]{0:T(512)S(1)} fusion(s32[1024]{0:T(1024)} %bitcast.73, f32[1024]{0:T(1024)} %bitcast.82, f32[]{:T(128)} %constant.48.clone.1), kind=kCustom, calls=%fused_computation.91 | custom fusion | flops 1024 | bytes 2560 | tf_op jit(solution)/shard_map/scatter-add | solution.py:100
  15.7 7.8 %scatter_custom_fusion.1 = f32[512]{0:T(512)S(1)} fusion(s32[1024]{0:T(1024)} %bitcast.77, f32[1024]{0:T(1024)} %bitcast.84, f32[]{:T(128)} %constant.48.clone.1), kind=kCustom, calls=%fused_computation.89 | custom fusion | flops 1024 | bytes 2560 | tf_op jit(solution)/shard_map/scatter-add | solution.py:100
  23.4 11.9 %psum.7 = f32[2,512]{1,0:T(2,128)S(1)} all-reduce(f32[2,512]{1,0:T(2,128)S(1)} %pad_maximum_fusion), channel_id=1, replica_groups=mesh['box'=128,'seg'=4] {'seg'}, use_global_device_ids=true, to_apply=%region_2.0 | all-reduce | flops 1024 | bytes 8192 | tf_op jit(solution)/shard_map/psum | solution.py:102
  35.3 0.7 broadcast_multiply_fusion.1
  36.0 0.7 fusion.43
  36.7 1.5 fusion.19
  38.2 1.8 fusion.4
  40.0 1.6 fusion.12
  41.6 1.8 fusion.13
  43.4 0.4 reshape.130
  43.7 0.7 convolution_bitcast_fusion.1
  44.5 0.0 copy-start
  44.5 0.5 copy.16
  45.0 1.1 all_gather_reshape.6
  46.1 0.0 all-gather.3.cloned.1.call-update
  46.1 0.0 all-gather.5.cloned.1.call-start
  46.2 0.0 copy-start.1
  46.2 39.5 %all-gather.3.cloned.1.call-done = f32[4,5,256,128]{3,2,1,0:T(8,128)} async-done(((f32[1,5,256,128]{3,2,1,0:T(8,128)}), f32[4,5,256,128]{3,2,1,0:T(8,128)}) %all-gather.3.cloned.1.call-update) | async-done | bytes 2621456 | tf_op jit(solution)/shard_map/all_gather | solution.py:74
  85.7 2.0 %reduce_sum.18 = f32[5,256,128]{2,1,0:T(8,128)S(1)} reduce(f32[4,5,256,128]{3,2,1,0:T(8,128)} %all-gather.3.cloned.1.call-done, f32[]{:T(128)} %constant.48.clone.1), dimensions={0}, to_apply=%region_3.4 | reduce | flops 491520 | bytes 3276804 | tf_op jit(solution)/shard_map/reduce_sum | solution.py:74
  87.7 7.9 %collective-permute-start = (f32[256,128]{1,0:T(8,128)S(1)}, f32[256,128]{1,0:T(8,128)S(1)}, u32[]{:S(2)}, u32[]{:S(2)}) collective-permute-start(f32[256,128]{1,0:T(8,128)S(1)} %get-tuple-element.50), channel_id=1, source_target_pairs={{8,0},{12,4},{16,8},{20,12},{24,16},{28,20},{32,24},{36,28},{40,32... | collective-permute-start | bytes 393224 | tf_op jit(solution)/shard_map/ppermute | solution.py:12
  95.5 1.9 %collective-permute-start.3 = (f32[256,128]{1,0:T(8,128)S(1)}, f32[256,128]{1,0:T(8,128)S(1)}, u32[]{:S(2)}, u32[]{:S(2)}) collective-permute-start(f32[256,128]{1,0:T(8,128)S(1)} %get-tuple-element.51), channel_id=1, source_target_pairs={{504,0},{508,4},{0,8},{4,12},{8,16},{12,20},{16,24},{20,28},{24,32... | collective-permute-start | bytes 393224 | tf_op jit(solution)/shard_map/ppermute | solution.py:12
  97.5 4.3 %collective-permute-start.2 = (f32[256,128]{1,0:T(8,128)S(1)}, f32[256,128]{1,0:T(8,128)S(1)}, u32[]{:S(2)}, u32[]{:S(2)}) collective-permute-start(f32[256,128]{1,0:T(8,128)S(1)} %get-tuple-element.52), channel_id=1, source_target_pairs={{508,0},{0,4},{4,8},{8,12},{12,16},{16,20},{20,24},{24,28},{28,32}... | collective-permute-start | bytes 393224 | tf_op jit(solution)/shard_map/ppermute | solution.py:12
  101.8 6.9 %collective-permute-start.1 = (f32[256,128]{1,0:T(8,128)S(1)}, f32[256,128]{1,0:T(8,128)S(1)}, u32[]{:S(2)}, u32[]{:S(2)}) collective-permute-start(f32[256,128]{1,0:T(8,128)S(1)} %get-tuple-element.53), channel_id=1, source_target_pairs={{4,0},{8,4},{12,8},{16,12},{20,16},{24,20},{28,24},{32,28},{36,32}... | collective-permute-start | bytes 393224 | tf_op jit(solution)/shard_map/ppermute | solution.py:12
  108.7 1.9 %collective-permute-done.2 = f32[256,128]{1,0:T(8,128)S(1)} collective-permute-done((f32[256,128]{1,0:T(8,128)S(1)}, f32[256,128]{1,0:T(8,128)S(1)}, u32[]{:S(2)}, u32[]{:S(2)}) %collective-permute-start.2) | collective-permute-done | bytes 131104 | tf_op jit(solution)/shard_map/ppermute | solution.py:12
  110.7 2.3 %collective-permute-done.1 = f32[256,128]{1,0:T(8,128)S(1)} collective-permute-done((f32[256,128]{1,0:T(8,128)S(1)}, f32[256,128]{1,0:T(8,128)S(1)}, u32[]{:S(2)}, u32[]{:S(2)}) %collective-permute-start.1) | collective-permute-done | bytes 131104 | tf_op jit(solution)/shard_map/ppermute | solution.py:12
  113.0 0.1 convert_element_type.82
  113.1 0.7 fusion.18
  113.8 1.8 fusion.1
  115.6 1.6 fusion.14
  117.2 1.8 fusion.15
  119.0 0.4 reshape.132
  119.4 0.7 convolution_bitcast_fusion
  120.1 0.5 copy.17
  120.6 1.1 all_gather_reshape.7
  121.7 0.0 all-gather.5.cloned.1.call-update
  121.7 34.0 %all-gather.5.cloned.1.call-done = f32[4,5,256,128]{3,2,1,0:T(8,128)} async-done(((f32[1,5,256,128]{3,2,1,0:T(8,128)}), f32[4,5,256,128]{3,2,1,0:T(8,128)}) %all-gather.5.cloned.1.call-update) | async-done | bytes 2621456 | tf_op jit(solution)/shard_map/all_gather | solution.py:74
  155.7 2.0 %reduce_sum.19 = f32[5,256,128]{2,1,0:T(8,128)S(1)} reduce(f32[4,5,256,128]{3,2,1,0:T(8,128)} %all-gather.5.cloned.1.call-done, f32[]{:T(128)} %constant.48.clone.1), dimensions={0}, to_apply=%region_4.5 | reduce | flops 491520 | bytes 3276804 | tf_op jit(solution)/shard_map/reduce_sum | solution.py:74
  157.7 7.9 %collective-permute-start.4 = (f32[256,128]{1,0:T(8,128)S(1)}, f32[256,128]{1,0:T(8,128)S(1)}, u32[]{:S(2)}, u32[]{:S(2)}) collective-permute-start(f32[256,128]{1,0:T(8,128)S(1)} %get-tuple-element.38), channel_id=1, source_target_pairs={{8,0},{12,4},{16,8},{20,12},{24,16},{28,20},{32,24},{36,28},{40,32... | collective-permute-start | bytes 393224 | tf_op jit(solution)/shard_map/ppermute | solution.py:12
  165.6 1.9 %collective-permute-start.7 = (f32[256,128]{1,0:T(8,128)S(1)}, f32[256,128]{1,0:T(8,128)S(1)}, u32[]{:S(2)}, u32[]{:S(2)}) collective-permute-start(f32[256,128]{1,0:T(8,128)S(1)} %get-tuple-element.39), channel_id=1, source_target_pairs={{504,0},{508,4},{0,8},{4,12},{8,16},{12,20},{16,24},{20,28},{24,32... | collective-permute-start | bytes 393224 | tf_op jit(solution)/shard_map/ppermute | solution.py:12
  167.5 4.3 %collective-permute-start.6 = (f32[256,128]{1,0:T(8,128)S(1)}, f32[256,128]{1,0:T(8,128)S(1)}, u32[]{:S(2)}, u32[]{:S(2)}) collective-permute-start(f32[256,128]{1,0:T(8,128)S(1)} %get-tuple-element.48), channel_id=1, source_target_pairs={{508,0},{0,4},{4,8},{8,12},{12,16},{16,20},{20,24},{24,28},{28,32}... | collective-permute-start | bytes 393224 | tf_op jit(solution)/shard_map/ppermute | solution.py:12
  171.8 6.7 %collective-permute-start.5 = (f32[256,128]{1,0:T(8,128)S(1)}, f32[256,128]{1,0:T(8,128)S(1)}, u32[]{:S(2)}, u32[]{:S(2)}) collective-permute-start(f32[256,128]{1,0:T(8,128)S(1)} %get-tuple-element.49), channel_id=1, source_target_pairs={{4,0},{8,4},{12,8},{16,12},{20,16},{24,20},{28,24},{32,28},{36,32}... | collective-permute-start | bytes 393224 | tf_op jit(solution)/shard_map/ppermute | solution.py:12
  178.5 0.7 copy.18
  179.2 1.4 collective-permute-done.6
  180.7 2.3 %collective-permute-done.5 = f32[256,128]{1,0:T(8,128)S(1)} collective-permute-done((f32[256,128]{1,0:T(8,128)S(1)}, f32[256,128]{1,0:T(8,128)S(1)}, u32[]{:S(2)}, u32[]{:S(2)}) %collective-permute-start.5) | collective-permute-done | bytes 131104 | tf_op jit(solution)/shard_map/ppermute | solution.py:12
  183.0 0.1 convert_element_type.91
  183.1 0.7 copy.19
  (18 shorter events, 0.2 us)
Async XLA Ops:
  7.2 78.5 %all-gather.3.cloned.1.call-start = ((), (), s32[]{:S(2)}) async-start(), calls=%async_computation | async-start | bytes 3276800 | tf_op jit(solution)/shard_map/all_gather | solution.py:74
  44.5 1.7 copy-start
  46.1 109.6 %all-gather.5.cloned.1.call-start = ((), (), s32[]{:S(2)}) async-start(), calls=%async_computation.1 | async-start | bytes 3276800 | tf_op jit(solution)/shard_map/all_gather | solution.py:74
  46.2 62.5 %copy-start.1 = (s32[1,1,1024]{2,1,0:T(1,128)S(1)}, s32[1,1,1024]{2,1,0:T(1,128)}, u32[]{:S(2)}) copy-start(s32[1,1,1024]{2,1,0:T(1,128)} %param.18) | copy-start | bytes 12292
  46.2 62.5 %copy-start.2 = (s32[1,1,1024]{2,1,0:T(1,128)S(1)}, s32[1,1,1024]{2,1,0:T(1,128)}, u32[]{:S(2)}) copy-start(s32[1,1,1024]{2,1,0:T(1,128)} %param.16) | copy-start | bytes 12292
  46.2 66.9 %copy-start.3 = (f32[1,1,1024]{2,1,0:T(1,128)S(1)}, f32[1,1,1024]{2,1,0:T(1,128)}, u32[]{:S(2)}) copy-start(f32[1,1,1024]{2,1,0:T(1,128)} %param.19) | copy-start | bytes 12292
  87.7 21.0 %collective-permute-start = (f32[256,128]{1,0:T(8,128)S(1)}, f32[256,128]{1,0:T(8,128)S(1)}, u32[]{:S(2)}, u32[]{:S(2)}) collective-permute-start(f32[256,128]{1,0:T(8,128)S(1)} %get-tuple-element.50), channel_id=1, source_target_pairs={{8,0},{12,4},{16,8},{20,12},{24,16},{28,20},{32,24},{36,28},{40,32... | collective-permute-start | bytes 393224 | tf_op jit(solution)/shard_map/ppermute | solution.py:12
  95.5 13.2 %collective-permute-start.3 = (f32[256,128]{1,0:T(8,128)S(1)}, f32[256,128]{1,0:T(8,128)S(1)}, u32[]{:S(2)}, u32[]{:S(2)}) collective-permute-start(f32[256,128]{1,0:T(8,128)S(1)} %get-tuple-element.51), channel_id=1, source_target_pairs={{504,0},{508,4},{0,8},{4,12},{8,16},{12,20},{16,24},{20,28},{24,32... | collective-permute-start | bytes 393224 | tf_op jit(solution)/shard_map/ppermute | solution.py:12
  97.5 13.2 %collective-permute-start.2 = (f32[256,128]{1,0:T(8,128)S(1)}, f32[256,128]{1,0:T(8,128)S(1)}, u32[]{:S(2)}, u32[]{:S(2)}) collective-permute-start(f32[256,128]{1,0:T(8,128)S(1)} %get-tuple-element.52), channel_id=1, source_target_pairs={{508,0},{0,4},{4,8},{8,12},{12,16},{16,20},{20,24},{24,28},{28,32}... | collective-permute-start | bytes 393224 | tf_op jit(solution)/shard_map/ppermute | solution.py:12
  101.8 11.2 %collective-permute-start.1 = (f32[256,128]{1,0:T(8,128)S(1)}, f32[256,128]{1,0:T(8,128)S(1)}, u32[]{:S(2)}, u32[]{:S(2)}) collective-permute-start(f32[256,128]{1,0:T(8,128)S(1)} %get-tuple-element.53), channel_id=1, source_target_pairs={{4,0},{8,4},{12,8},{16,12},{20,16},{24,20},{28,24},{32,28},{36,32}... | collective-permute-start | bytes 393224 | tf_op jit(solution)/shard_map/ppermute | solution.py:12
  157.7 21.5 %collective-permute-start.4 = (f32[256,128]{1,0:T(8,128)S(1)}, f32[256,128]{1,0:T(8,128)S(1)}, u32[]{:S(2)}, u32[]{:S(2)}) collective-permute-start(f32[256,128]{1,0:T(8,128)S(1)} %get-tuple-element.38), channel_id=1, source_target_pairs={{8,0},{12,4},{16,8},{20,12},{24,16},{28,20},{32,24},{36,28},{40,32... | collective-permute-start | bytes 393224 | tf_op jit(solution)/shard_map/ppermute | solution.py:12
  165.6 13.7 %collective-permute-start.7 = (f32[256,128]{1,0:T(8,128)S(1)}, f32[256,128]{1,0:T(8,128)S(1)}, u32[]{:S(2)}, u32[]{:S(2)}) collective-permute-start(f32[256,128]{1,0:T(8,128)S(1)} %get-tuple-element.39), channel_id=1, source_target_pairs={{504,0},{508,4},{0,8},{4,12},{8,16},{12,20},{16,24},{20,28},{24,32... | collective-permute-start | bytes 393224 | tf_op jit(solution)/shard_map/ppermute | solution.py:12
  167.5 13.2 %collective-permute-start.6 = (f32[256,128]{1,0:T(8,128)S(1)}, f32[256,128]{1,0:T(8,128)S(1)}, u32[]{:S(2)}, u32[]{:S(2)}) collective-permute-start(f32[256,128]{1,0:T(8,128)S(1)} %get-tuple-element.48), channel_id=1, source_target_pairs={{508,0},{0,4},{4,8},{8,12},{12,16},{16,20},{20,24},{24,28},{28,32}... | collective-permute-start | bytes 393224 | tf_op jit(solution)/shard_map/ppermute | solution.py:12
  171.8 11.2 %collective-permute-start.5 = (f32[256,128]{1,0:T(8,128)S(1)}, f32[256,128]{1,0:T(8,128)S(1)}, u32[]{:S(2)}, u32[]{:S(2)}) collective-permute-start(f32[256,128]{1,0:T(8,128)S(1)} %get-tuple-element.49), channel_id=1, source_target_pairs={{4,0},{8,4},{12,8},{16,12},{20,16},{24,20},{28,24},{32,28},{36,32}... | collective-permute-start | bytes 393224 | tf_op jit(solution)/shard_map/ppermute | solution.py:12
Sparse Core Ops, SparseCore 0:
  46.2 39.4 all-gather.2
  121.8 33.8 all-gather.4
